TPU v7x, 128 devices: a whole 4x4x4 slice. The times are simulated.
128 devices in a mesh: wide: 32 (over y, x, core), samp: 4 (over z).
Axes of the slice: x: 4, y: 4, z: 4, core: 2. Of those that a mesh axis runs over, the one named last changes fastest.
Arguments:
- features: bfloat16 [4, 128, 96, 128], P('samp', 'wide'), may hold values from -6 to 6
- labels: int32 [4, 128, 96], P('samp', 'wide'), may hold values from 0 to 8
- conv_weight: bfloat16 [3, 3, 128, 128], replicated, may hold values from -0.1875 to 0.1875
- down_weight: bfloat16 [512, 1024], replicated, may hold values from -0.25 to 0.25
- expand_weight: bfloat16 [3, 3, 1024, 2048], P(None, None, None, 'wide'), may hold values from -0.0625 to 0.0625
- reduce_weight: bfloat16 [3, 3, 2048, 1024], P(None, None, 'wide'), may hold values from -0.046875 to 0.046875
- up_weight: bfloat16 [1024, 512], replicated, may hold values from -0.1875 to 0.1875
- class_weight: bfloat16 [128, 9], replicated, may hold values from -3 to 3
Outputs:
- conv_grad: float32 [3, 3, 128, 128], replicated
- down_grad: float32 [512, 1024], replicated
- expand_grad: float32 [3, 3, 1024, 2048], P(None, None, 'samp', 'wide')
- reduce_grad: float32 [3, 3, 2048, 1024], P(None, None, 'wide', 'samp')
- up_grad: float32 [1024, 512], replicated
- class_grad: float32 [128, 9], replicated
All inputs are finite; a program needn't handle non-finite values.
Results may differ from a plain program's by a relative error of at most 0.012.
Values may be sent and summed in bfloat16 or wider, within the bound.
A program may use at most 192 MiB of HBM per device.

v0:
```python
import math
import jax
import jax.numpy as jnp
from jax import lax
from jax.sharding import PartitionSpec as P


def split_up(x, dim, length):
    before, after = (x.shape[:dim], x.shape[dim + 1 :])
    return jnp.moveaxis(x.reshape(*before, length, -1, *after), dim, 0)


def sum_at_owner(x, axis, dim):
    length = lax.axis_size(axis)
    pieces = lax.all_to_all(split_up(x, dim, length), axis, 0, 0, tiled=True)
    return jnp.sum(pieces.astype(jnp.float32), axis=0)


def extended(block, sides, width):
    for axis, dim in sides:
        count = lax.axis_size(axis)
        forward = [(i, i + 1) for i in range(count - 1)]
        backward = [(target, source) for source, target in forward]
        low = lax.ppermute(
            lax.slice_in_dim(block, block.shape[dim] - width, None, axis=dim), axis, forward
        )
        high = lax.ppermute(lax.slice_in_dim(block, 0, width, axis=dim), axis, backward)
        block = jnp.concatenate([low, block, high], axis=dim)
    return block


def silu_slope(value):
    logistic = jax.nn.sigmoid(value)
    return logistic * (1.0 + value * (1.0 - logistic))


def pad_both(values):
    return jnp.pad(values, ((1, 1), (1, 1), (0, 0)))


def to_depth(grid):
    height, across, channels = grid.shape
    blocks = grid.reshape(height // 2, 2, across // 2, 2, channels)
    return jnp.transpose(blocks, (0, 2, 1, 3, 4)).reshape(height // 2, across // 2, 4 * channels)


def from_depth(grid):
    height, across, channels = grid.shape
    blocks = grid.reshape(height, across, 2, 2, channels // 4)
    return jnp.transpose(blocks, (0, 2, 1, 3, 4)).reshape(2 * height, 2 * across, channels // 4)


def taps_in(padded, height, across):
    return jnp.concatenate(
        [padded[p : p + height, q : q + across] for p in range(3) for q in range(3)], axis=-1
    )


def taps_out(values):
    return jnp.concatenate(
        [jnp.pad(values, ((p, 2 - p), (q, 2 - q), (0, 0))) for p in range(3) for q in range(3)],
        axis=-1,
    )


def conv_padded(padded, weight):
    height = padded.shape[0] - 2
    across = padded.shape[1] - 2
    inward = weight.shape[2]
    outward = weight.shape[3]
    if inward <= outward:
        window = taps_in(padded, height, across).reshape(height * across, 9 * inward)
        result = jnp.dot(
            window, weight.reshape(9 * inward, outward), preferred_element_type=jnp.float32
        )
        return result.reshape(height, across, outward)
    flattened = padded.reshape((height + 2) * (across + 2), inward)
    stacked = jnp.transpose(weight, (2, 0, 1, 3)).reshape(inward, 9 * outward)
    spread_out = jnp.dot(flattened, stacked, preferred_element_type=jnp.float32).reshape(
        height + 2, across + 2, 9, outward
    )
    summed = spread_out[0:height, 0:across, 0]
    for offset in range(1, 9):
        p = offset // 3
        q = offset % 3
        summed = summed + spread_out[p : p + height, q : q + across, offset]
    return summed


def correlate(padded, values):
    height, across, outward = values.shape
    inward = padded.shape[-1]
    if inward <= outward:
        window = taps_in(padded, height, across).reshape(height * across, 9 * inward)
        result = lax.dot_general(
            window,
            values.reshape(height * across, outward),
            (((0,), (0,)), ((), ())),
            preferred_element_type=jnp.float32,
        )
        return result.reshape(3, 3, inward, outward)
    shifted = taps_out(values).reshape((height + 2) * (across + 2), 9 * outward)
    result = lax.dot_general(
        padded.reshape(-1, inward),
        shifted,
        (((0,), (0,)), ((), ())),
        preferred_element_type=jnp.float32,
    )
    return jnp.transpose(result.reshape(inward, 3, 3, outward), (1, 2, 0, 3))


def contract_rows(left, right):
    left_flat = left.reshape(-1, left.shape[-1])
    right_flat = right.reshape(-1, right.shape[-1])
    return lax.dot_general(
        left_flat, right_flat, (((0,), (0,)), ((), ())), preferred_element_type=jnp.float32
    )


def flip_kernel(weight):
    return jnp.transpose(weight[::-1, ::-1], (0, 1, 3, 2))


def keep_rows(block_rows, first_row):
    return block_rows


def project_rows(values, weight):
    return jnp.dot(values, weight, preferred_element_type=jnp.float32).astype(jnp.bfloat16)


def widen_rows(values, weight):
    return lax.dot_general(
        values, weight, (((2,), (1,)), ((), ())), preferred_element_type=jnp.float32
    ).astype(jnp.bfloat16)


def collect(values, transform):
    return transform(lax.all_gather(values, "wide", axis=0, tiled=True), jnp.int32(0))


def spread_sum(term_rows, row_total):
    return sum_at_owner(
        term_rows(jnp.int32(0), row_total * lax.axis_size("wide")).astype(jnp.bfloat16), "wide", 0
    )


def local(
    features,
    labels,
    conv_weight,
    down_weight,
    expand_weight,
    reduce_weight,
    up_weight,
    class_weight,
):
    crop_rows = features[0]
    label_map = labels[0]
    height, across, channels = crop_rows.shape
    half_rows = height // 2
    pixel_count = lax.axis_size("wide") * lax.axis_size("samp") * height * across
    loss_scale = 8.0 / math.sqrt(pixel_count)
    classes = lax.broadcasted_iota(jnp.int32, (1, 1, class_weight.shape[1]), 2)
    near_rows = extended(crop_rows, (("wide", 0),), 1)
    padded_in = jnp.pad(near_rows, ((0, 0), (1, 1), (0, 0)))
    hidden_pre = conv_padded(padded_in, conv_weight)
    hidden = jax.nn.silu(hidden_pre).astype(jnp.bfloat16)
    stacked = to_depth(hidden)
    coarse = project_rows(stacked, down_weight)
    coarse_all = collect(coarse, keep_rows)
    coarse_pad = pad_both(coarse_all)
    expand_pre = conv_padded(coarse_pad, expand_weight)
    expanded = jax.nn.silu(expand_pre).astype(jnp.bfloat16)
    expand_pad = pad_both(expanded)

    def reduce_block(first_row, row_count):
        return conv_padded(expand_pad, reduce_weight)

    bottom = (coarse.astype(jnp.float32) + spread_sum(reduce_block, half_rows)).astype(jnp.bfloat16)
    upward = from_depth(jnp.dot(bottom, up_weight, preferred_element_type=jnp.float32))
    joined_pre = upward + hidden.astype(jnp.float32)
    joined = jax.nn.silu(joined_pre).astype(jnp.bfloat16)
    logits = jnp.dot(joined, class_weight, preferred_element_type=jnp.float32)
    exp_logits = jnp.exp(logits)
    probability = exp_logits / jnp.sum(exp_logits, axis=-1, keepdims=True)
    onehot = (label_map[:, :, None] == classes).astype(jnp.float32)
    logit_grad = ((probability - onehot) * loss_scale).astype(jnp.bfloat16)
    class_grad = contract_rows(joined, logit_grad)
    joined_grad = lax.dot_general(
        logit_grad, class_weight, (((2,), (1,)), ((), ())), preferred_element_type=jnp.float32
    )
    upward_grad = (joined_grad * silu_slope(joined_pre)).astype(jnp.bfloat16)
    stacked_grad = to_depth(upward_grad)
    up_grad = contract_rows(bottom, stacked_grad)
    bottom_grad = widen_rows(stacked_grad, up_weight)
    bottom_all = collect(bottom_grad, keep_rows)
    reduce_grad = correlate(expand_pad, bottom_all)
    expanded_back = conv_padded(pad_both(bottom_all), flip_kernel(reduce_weight))
    expanded_grad = (expanded_back * silu_slope(expand_pre)).astype(jnp.bfloat16)
    expand_grad = correlate(coarse_pad, expanded_grad)
    grad_pad = pad_both(expanded_grad)
    back_expand = flip_kernel(expand_weight)

    def expand_back_block(first_row, row_count):
        return conv_padded(grad_pad, back_expand)

    coarse_grad = (
        bottom_grad.astype(jnp.float32) + spread_sum(expand_back_block, half_rows)
    ).astype(jnp.bfloat16)
    down_grad = contract_rows(stacked, coarse_grad)
    down_back = lax.dot_general(
        coarse_grad, down_weight, (((2,), (1,)), ((), ())), preferred_element_type=jnp.float32
    )
    hidden_sum = from_depth(down_back) + upward_grad.astype(jnp.float32)
    hidden_grad = (hidden_sum * silu_slope(hidden_pre)).astype(jnp.bfloat16)
    conv_grad = correlate(padded_in, hidden_grad)
    conv_grad, down_grad, up_grad, class_grad = lax.psum(
        (conv_grad, down_grad, up_grad, class_grad), ("wide", "samp")
    )
    expand_grad, reduce_grad = (
        sum_at_owner(expand_grad.astype(jnp.bfloat16), "samp", 2),
        sum_at_owner(reduce_grad.astype(jnp.bfloat16), "samp", 3),
    )
    return (conv_grad, down_grad, expand_grad, reduce_grad, up_grad, class_grad)


def solution(mesh):
    return jax.shard_map(
        local,
        mesh=mesh,
        in_specs=(
            P("samp", "wide", None, None),
            P("samp", "wide", None),
            P(),
            P(),
            P(None, None, None, "wide"),
            P(None, None, "wide", None),
            P(),
            P(),
        ),
        out_specs=(
            P(),
            P(),
            P(None, None, "samp", "wide"),
            P(None, None, "wide", "samp"),
            P(),
            P(),
        ),
        check_vma=False,
    )
```

profile of v0, /device:TPU:1, one launch (start us, length us, event | category | flops | bytes accessed | tf_op | source)
XLA Modules:
  0.0 589.7 jit_solution(12321008439119090654)
XLA Ops:
  8.1 4.5 collective-permute-start
  12.6 1.9 collective-permute-start.1
  14.5 3.2 collective-permute-done.1
  18.7 1.6 constant_dynamic-update-slice_fusion.16
  21.3 1.5 constant_dynamic-update-slice_fusion.10
  23.7 2.0 multiply_convert_fusion.3
  25.9 2.2 convolution_convert_fusion.4
  28.2 52.9 %all-gather.3.cloned.1.call-done = bf16[64,48,1024]{2,1,0:T(8,128)(2,1)} async-done(((bf16[2,48,1024]{2,1,0:T(8,128)(2,1)}), bf16[64,48,1024]{2,1,0:T(8,128)(2,1)}) %all-gather.3.cloned.1.call-update) | async-done | bytes 6291472 | tf_op jit(solution)/shard_map/all_gather | solution.py:139
  81.1 6.3 %copy.56 = bf16[64,48,1024]{2,0,1:T(8,128)(2,1)S(1)} copy(bf16[64,48,1024]{2,1,0:T(8,128)(2,1)} %all-gather.3.cloned.1.call-done) | data formatting | bytes 12582912 | tf_op jit(solution)/shard_map/all_gather | solution.py:139
  87.4 11.4 %fusion.1 = f32[66,50,9,64]{0,3,2,1:T(8,128)} fusion(bf16[9,64,1024,1]{2,1,0,3:T(8,128)(2,1)S(1)} %bitcast.176, bf16[64,48,1024]{2,0,1:T(8,128)(2,1)S(1)} %copy.56), kind=kOutput, calls=%fused_computation.3 | convolution fusion | flops 3892838400 | bytes 15074304 | tf_op jit(solution)/shard_map/dot_general | solution.py:79
  98.8 7.6 %multiply_convert_fusion = (bf16[64,48,64]{0,2,1:T(8,128)(2,1)S(1)}, f32[64,48,64]{0,2,1:T(8,128)S(1)}) fusion(f32[66,50,9,64]{0,3,2,1:T(8,128)} %fusion.1), kind=kLoop, calls=%fused_computation.34 | loop fusion | flops 2555904 | bytes 8257536 | tf_op jit(solution)/shard_map/convert_element_type | solution.py:174
  106.5 1.2 slice_dynamic-update-slice_fusion.15
  107.7 1.3 slice_dynamic-update-slice_fusion.14
  109.0 1.3 slice_dynamic-update-slice_fusion.13
  113.5 1.2 slice_dynamic-update-slice_fusion.10
  114.8 1.2 slice_dynamic-update-slice_fusion.9
  116.0 1.2 slice_dynamic-update-slice_fusion.8
  117.2 10.7 %copy.57 = bf16[64,48,576]{2,1,0:T(8,128)(2,1)} copy(bf16[64,48,576]{0,2,1:T(8,128)(2,1)} %slice_dynamic-update-slice_fusion.8) | data formatting | bytes 7077888 | tf_op jit(solution)/shard_map/concatenate | solution.py:54
  127.9 7.1 %convolution_convert_fusion.1 = bf16[64,48,1024]{2,1,0:T(8,128)(2,1)S(1)} fusion(bf16[64,48,576]{2,1,0:T(8,128)(2,1)} %copy.57, bf16[576,1024,1]{1,0,2:T(8,128)(2,1)} %bitcast.177), kind=kOutput, calls=%fused_computation.11 | convolution fusion | flops 3627024384 | bytes 11010048 | tf_op jit(solution)/shard_map/dot_general | solution.py:73
  135.0 78.0 %all_to_all.20 = bf16[32,2,48,1024]{3,2,1,0:T(8,128)(2,1)S(1)} all-to-all(bf16[32,2,48,1024]{3,2,1,0:T(8,128)(2,1)S(1)} %bitcast.166), channel_id=1, replica_groups=mesh['wide'=32,'samp'=4] {'wide'}, dimensions={0} | all-to-all | bytes 12582912 | tf_op jit(solution)/shard_map/all_to_all | solution.py:15
  213.1 1.5 convert_reduce_fusion.1
  217.4 2.4 rev.7
  219.8 2.4 rev.6
  222.2 43.3 %all-gather.5.cloned.1.call-done = bf16[64,48,1024]{2,1,0:T(8,128)(2,1)} async-done(((bf16[2,48,1024]{2,1,0:T(8,128)(2,1)}), bf16[64,48,1024]{2,1,0:T(8,128)(2,1)}) %all-gather.5.cloned.1.call-update) | async-done | bytes 6291472 | tf_op jit(solution)/shard_map/all_gather | solution.py:139
  265.4 6.4 %copy.60 = bf16[64,48,1024]{2,0,1:T(8,128)(2,1)S(1)} copy(bf16[64,48,1024]{2,1,0:T(8,128)(2,1)} %all-gather.5.cloned.1.call-done) | data formatting | bytes 12582912 | tf_op jit(solution)/shard_map/all_gather | solution.py:139
  271.9 8.4 %fusion.3 = f32[66,50,9,64]{0,3,1,2:T(8,128)S(1)} fusion(bf16[9,64,1024,1]{2,1,3,0:T(8,128)(2,1)S(1)} %bitcast.179, bf16[64,48,1024]{2,0,1:T(8,128)(2,1)S(1)} %copy.60), kind=kOutput, calls=%fused_computation.5 | convolution fusion | flops 3892838400 | bytes 15074304 | tf_op jit(solution)/shard_map/dot_general | solution.py:79
  280.2 2.6 fusion.10
  282.9 1.2 slice_dynamic-update-slice_fusion.7
  284.1 1.3 slice_dynamic-update-slice_fusion.6
  285.4 1.3 slice_dynamic-update-slice_fusion.5
  289.9 1.2 slice_dynamic-update-slice_fusion.2
  291.1 1.2 slice_dynamic-update-slice_fusion.1
  292.4 1.2 slice_dynamic-update-slice_fusion
  293.6 10.7 %copy.70 = bf16[64,48,576]{2,1,0:T(8,128)(2,1)} copy(bf16[64,48,576]{0,2,1:T(8,128)(2,1)} %slice_dynamic-update-slice_fusion) | data formatting | bytes 7077888 | tf_op jit(solution)/shard_map/concatenate | solution.py:54
  304.3 9.1 %convolution_convert_fusion = bf16[64,48,1024]{2,1,0:T(8,128)(2,1)} fusion(bf16[64,48,576]{2,1,0:T(8,128)(2,1)} %copy.70, bf16[576,1024,1]{1,0,2:T(8,128)(2,1)S(1)} %bitcast.178), kind=kOutput, calls=%fused_computation.10 | convolution fusion | flops 3627024384 | bytes 11010048 | tf_op jit(solution)/shard_map/dot_general | solution.py:73
  313.4 5.4 all-to-all-start.1
  320.8 6.3 %copy.91 = bf16[64,48,1024]{2,1,0:T(8,128)(2,1)S(1)} copy(bf16[64,48,1024]{2,0,1:T(8,128)(2,1)} %copy-done.2) | data formatting | bytes 12582912
  327.1 7.7 %pad.52.clone = bf16[66,50,1024]{2,1,0:T(8,128)(2,1)} pad(bf16[64,48,1024]{2,1,0:T(8,128)(2,1)S(1)} %copy.91, bf16[]{:T(256)} %constant.4.clone.1), padding=1_1x1_1x0_0 | pad | bytes 13049858 | tf_op jit(solution)/shard_map/jit(_pad)/pad | solution.py:38
  334.8 9.4 %reshape.180 = bf16[3300,1024,1,1]{1,0,2,3:T(8,128)(2,1)} reshape(bf16[66,50,1024]{2,1,0:T(8,128)(2,1)} %pad.52.clone) | data formatting | bytes 13516800 | tf_op jit(solution)/shard_map/reshape | solution.py:77
  344.2 6.2 %copy.77 = bf16[576,3072]{1,0:T(8,128)(2,1)} copy(bf16[576,3072]{0,1:T(8,128)(2,1)} %bitcast.163) | data formatting | bytes 7077888 | tf_op jit(solution)/shard_map/dot_general | solution.py:95
  350.4 1.8 fusion.50
  352.2 7.7 %convolution_convert_fusion.2 = bf16[3,3,64,1024]{3,2,1,0:T(8,128)(2,1)S(1)} fusion(bf16[3,3,64,3072]{3,2,1,0:T(8,128)(2,1)} %bitcast.168, bf16[3072,1024,1,1]{1,0,3,2:T(8,128)(2,1)} %bitcast.164), kind=kOutput, calls=%fused_computation.37 | convolution fusion | flops 3624468480 | bytes 11010048 | tf_op jit(solution)/shard_map/dot_general | solution.py:95
  359.9 1.2 copy.92
  362.2 1.2 pad_dynamic-update-slice_fusion.6
  364.5 1.3 pad_dynamic-update-slice_fusion.4
  365.8 1.3 pad_dynamic-update-slice_fusion.8
  367.0 1.3 pad_dynamic-update-slice_fusion.3
  368.3 1.3 pad_dynamic-update-slice_fusion.2
  369.6 1.3 pad_dynamic-update-slice_fusion.1
  370.8 1.2 pad_dynamic-update-slice_fusion
  372.1 12.9 %copy.73 = bf16[66,50,576]{2,1,0:T(8,128)(2,1)} copy(bf16[66,50,576]{0,2,1:T(8,128)(2,1)} %pad_dynamic-update-slice_fusion) | data formatting | bytes 7603200 | tf_op jit(solution)/shard_map/concatenate | solution.py:60
  385.0 7.9 %reshape.155 = bf16[3300,576]{1,0:T(8,128)(2,1)} reshape(bf16[66,50,576]{2,1,0:T(8,128)(2,1)} %copy.73) | data formatting | bytes 7603200 | tf_op jit(solution)/shard_map/reshape | solution.py:102
  392.9 6.4 %copy.74 = bf16[576,3300]{1,0:T(8,128)(2,1)} copy(bf16[576,3300]{0,1:T(8,128)(2,1)} %bitcast.162) | data formatting | bytes 7603200 | tf_op jit(solution)/shard_map/dot_general | solution.py:103
  399.3 4.3 all-to-all-start.3
  403.8 4.3 convert_reduce_fusion
  410.0 1.2 fusion.48
  411.2 2.7 fusion.49
  413.9 8.2 %fusion.12 = bf16[1024,3,3,64]{0,3,2,1:T(8,128)(2,1)S(1)} fusion(bf16[3,3,64,3300]{3,2,1,0:T(8,128)(2,1)} %bitcast.167, bf16[3300,1024,1,1]{1,0,2,3:T(8,128)(2,1)} %reshape.180), kind=kOutput, calls=%fused_computation.36 | convolution fusion | flops 3893428224 | bytes 11739648 | tf_op jit(solution)/shard_map/dot_general | solution.py:103
  423.2 4.2 all-to-all-start.2
  427.7 77.0 %psum.31 = f32[128,9]{0,1:T(8,128)} all-reduce(f32[128,9]{0,1:T(8,128)S(1)} %convolution_bitcast_fusion), channel_id=1, replica_groups=mesh['wide'=32,'samp'=4] {'wide','samp'}, use_global_device_ids=true, to_apply=%region_8.9 | all-reduce | flops 1152 | bytes 9216 | tf_op jit(solution)/shard_map/psum | solution.py:218
  506.7 69.6 %all-reduce.16.cloned.1.call-done = (f32[3,3,128,128]{3,2,1,0:T(8,128)}, f32[512,1024]{1,0:T(8,128)}, f32[1024,512]{1,0:T(8,128)}) async-done(((f32[3,3,128,128]{3,2,1,0:T(8,128)}, f32[512,1024]{1,0:T(8,128)}, f32[1024,512]{1,0:T(8,128)}), (f32[3,3,128,128]{3,2,1,0:T(8,128)}, f32[512,1024]{1,0:T(8,128)}, f32[1024,512]{1,0:T(8,128)})) %all-reduce.16.cloned.1.call-update) | async-done | bytes 4784144 | tf_op jit(solution)/shard_map/psum | solution.py:218
  576.3 2.1 copy.139
  578.4 3.2 copy.140
  581.6 1.3 copy.141
  (106 shorter events, 22.9 us)
Async XLA Ops:
  7.2 207.5 %copy-start = (bf16[1024,512]{1,0:T(8,128)(2,1)S(1)}, bf16[1024,512]{1,0:T(8,128)(2,1)}, u32[]{:S(2)}) copy-start(bf16[1024,512]{1,0:T(8,128)(2,1)} %param.14) | copy-start | bytes 3145732
  7.2 73.9 %all-gather.3.cloned.1.call-start = ((), (), s32[]{:S(2)}) async-start(), calls=%async_computation.4 | async-start | bytes 6488064 | tf_op jit(solution)/shard_map/all_gather | solution.py:139
  8.1 6.4 %collective-permute-start = (bf16[1,96,128]{2,1,0:T(8,128)(2,1)S(1)}, bf16[1,96,128]{2,1,0:T(8,128)(2,1)S(1)}, u32[]{:S(2)}, u32[]{:S(2)}) collective-permute-start(bf16[1,96,128]{2,1,0:T(8,128)(2,1)S(1)} %get-tuple-element.22), channel_id=1, source_target_pairs={{0,4},{4,8},{8,12},{12,16},{16,20},{20,24},{24,28},{28,32},{32,36}... | collective-permute-start | bytes 73736 | tf_op jit(solution)/shard_map/ppermute | solution.py:24
  12.6 5.1 collective-permute-start.1
  28.1 59.3 %copy-start.8 = (bf16[3,3,1024,64]{2,3,1,0:T(8,128)(2,1)S(1)}, bf16[3,3,1024,64]{2,3,1,0:T(8,128)(2,1)}, u32[]{:S(2)}) copy-start(bf16[3,3,1024,64]{2,3,1,0:T(8,128)(2,1)} %param.12) | copy-start | bytes 3538948
  28.1 237.3 %all-gather.5.cloned.1.call-start = ((), (), s32[]{:S(2)}) async-start(), calls=%async_computation.5 | async-start | bytes 6488064 | tf_op jit(solution)/shard_map/all_gather | solution.py:139
  87.4 11.4 %copy-start.2 = (bf16[64,48,1024]{2,0,1:T(8,128)(2,1)}, bf16[64,48,1024]{2,0,1:T(8,128)(2,1)S(1)}, u32[]{:S(2)}) copy-start(bf16[64,48,1024]{2,0,1:T(8,128)(2,1)S(1)} %copy.56) | copy-start | bytes 18874372
  213.1 1.5 copy-start.7
  213.1 2.2 copy-start.21
  213.1 2.9 copy-start.22
  215.3 0.6 copy-start.19
  216.2 55.7 %copy-start.11 = (bf16[4,96,128]{2,1,0:T(8,128)(2,1)}, bf16[4,96,128]{2,1,0:T(8,128)(2,1)S(1)}, u32[]{:S(2)}) copy-start(bf16[4,96,128]{2,1,0:T(8,128)(2,1)S(1)} %fusion.15) | copy-start | bytes 294916
  265.4 6.4 %copy-start.10 = (bf16[3,3,64,1024]{3,2,1,0:T(8,128)(2,1)S(1)}, bf16[3,3,64,1024]{3,2,1,0:T(8,128)(2,1)}, u32[]{:S(2)}) copy-start(bf16[3,3,64,1024]{3,2,1,0:T(8,128)(2,1)} %rev.6) | copy-start | bytes 3538948
  292.4 11.9 %copy-start.9 = (bf16[3,3,1024,64]{2,3,1,0:T(8,128)(2,1)S(1)}, bf16[3,3,1024,64]{2,3,1,0:T(8,128)(2,1)}, u32[]{:S(2)}) copy-start(bf16[3,3,1024,64]{2,3,1,0:T(8,128)(2,1)} %rev.7) | copy-start | bytes 3538948
  313.4 6.2 %copy-start.16 = (bf16[4,96,128]{2,1,0:T(8,128)(2,1)S(1)}, bf16[4,96,128]{2,1,0:T(8,128)(2,1)}, u32[]{:S(2)}) copy-start(bf16[4,96,128]{2,1,0:T(8,128)(2,1)} %get-tuple-element.20) | copy-start | bytes 294916
  313.4 6.2 %copy-start.18 = (bf16[4,96,128]{2,1,0:T(8,128)(2,1)S(1)}, bf16[4,96,128]{2,1,0:T(8,128)(2,1)}, u32[]{:S(2)}) copy-start(bf16[4,96,128]{2,1,0:T(8,128)(2,1)} %get-tuple-element.14) | copy-start | bytes 294916
  313.4 6.2 %copy-start.15 = (bf16[4,96,128]{2,1,0:T(8,128)(2,1)S(1)}, bf16[4,96,128]{2,1,0:T(8,128)(2,1)}, u32[]{:S(2)}) copy-start(bf16[4,96,128]{2,1,0:T(8,128)(2,1)} %get-tuple-element.19) | copy-start | bytes 294916
  313.4 6.3 %copy-start.14 = (bf16[4,96,128]{2,1,0:T(8,128)(2,1)S(1)}, bf16[4,96,128]{2,1,0:T(8,128)(2,1)}, u32[]{:S(2)}) copy-start(bf16[4,96,128]{2,1,0:T(8,128)(2,1)} %get-tuple-element.18) | copy-start | bytes 294916
  313.4 6.3 %copy-start.4 = (bf16[1,4,96,128]{3,2,1,0:T(8,128)(2,1)S(1)}, bf16[1,4,96,128]{3,2,1,0:T(8,128)(2,1)}, u32[]{:S(2)}) copy-start(bf16[1,4,96,128]{3,2,1,0:T(8,128)(2,1)} %param.8) | copy-start | bytes 294916
  313.4 6.3 %copy-start.13 = (bf16[4,96,128]{2,1,0:T(8,128)(2,1)S(1)}, bf16[4,96,128]{2,1,0:T(8,128)(2,1)}, u32[]{:S(2)}) copy-start(bf16[4,96,128]{2,1,0:T(8,128)(2,1)} %get-tuple-element.17) | copy-start | bytes 294916
  313.4 6.4 %copy-start.12 = (bf16[4,96,128]{2,1,0:T(8,128)(2,1)S(1)}, bf16[4,96,128]{2,1,0:T(8,128)(2,1)}, u32[]{:S(2)}) copy-start(bf16[4,96,128]{2,1,0:T(8,128)(2,1)} %get-tuple-element.16) | copy-start | bytes 294916
  313.4 6.4 %copy-start.17 = (bf16[4,96,128]{2,1,0:T(8,128)(2,1)S(1)}, bf16[4,96,128]{2,1,0:T(8,128)(2,1)}, u32[]{:S(2)}) copy-start(bf16[4,96,128]{2,1,0:T(8,128)(2,1)} %get-tuple-element.12) | copy-start | bytes 294916
  313.4 85.8 %all-to-all-start.1 = ((bf16[32,2,48,1024]{3,2,1,0:T(8,128)(2,1)}), bf16[32,2,48,1024]{3,2,1,0:T(8,128)(2,1)}, u32[]{:S(2)}, u32[]{:S(2)}) async-start(bf16[32,2,48,1024]{3,2,1,0:T(8,128)(2,1)} %bitcast.165), calls=%async_computation.1 | async-start | bytes 12582912 | tf_op jit(solution)/shard_map/all_to_all | solution.py:15
  399.2 8.9 %copy-start.6 = (bf16[2,48,1024]{2,1,0:T(8,128)(2,1)S(1)}, bf16[2,48,1024]{2,1,0:T(8,128)(2,1)}, u32[]{:S(2)}) copy-start(bf16[2,48,1024]{2,1,0:T(8,128)(2,1)} %convolution_convert_fusion.3) | copy-start | bytes 589828
  399.2 9.0 %copy-start.3 = (bf16[512,1024]{1,0:T(8,128)(2,1)S(1)}, bf16[512,1024]{1,0:T(8,128)(2,1)}, u32[]{:S(2)}) copy-start(bf16[512,1024]{1,0:T(8,128)(2,1)} %param.11) | copy-start | bytes 3145732
  399.3 24.0 %all-to-all-start.3 = ((bf16[4,3,3,64,256]{4,3,2,1,0:T(8,128)(2,1)}), bf16[4,3,3,64,256]{4,3,2,1,0:T(8,128)(2,1)S(1)}, u32[]{:S(2)}, u32[]{:S(2)}) async-start(bf16[4,3,3,64,256]{4,3,2,1,0:T(8,128)(2,1)} %bitcast.157), calls=%async_computation.3 | async-start | bytes 2359296 | tf_op jit(solution)/shard_map/all_to_all | solution.py:15
  403.5 172.8 %all-reduce.16.cloned.1.call-start = ((), (), s32[]{:S(2)}) async-start(), calls=%async_computation.6 | async-start | bytes 9568256 | tf_op jit(solution)/shard_map/psum | solution.py:218
  413.9 13.6 %copy-start.20 = (bf16[4,96,128]{2,1,0:T(8,128)(2,1)S(1)}, bf16[4,96,128]{2,1,0:T(8,128)(2,1)}, u32[]{:S(2)}) copy-start(bf16[4,96,128]{2,1,0:T(8,128)(2,1)} %copy-done.19) | copy-start | bytes 294916
  423.2 82.5 %all-to-all-start.2 = ((bf16[4,3,3,256,64]{3,4,2,1,0:T(8,128)(2,1)}), bf16[4,3,3,256,64]{3,4,2,1,0:T(8,128)(2,1)S(1)}, u32[]{:S(2)}, u32[]{:S(2)}) async-start(bf16[4,3,3,256,64]{3,4,2,1,0:T(8,128)(2,1)} %bitcast.159), calls=%async_computation.2 | async-start | bytes 2359296 | tf_op jit(solution)/shard_map/all_to_all | solution.py:15
  427.7 155.2 %copy-start.1 = (bf16[1024,512]{1,0:T(8,128)(2,1)S(1)}, bf16[1024,512]{1,0:T(8,128)(2,1)}, u32[]{:S(2)}) copy-start(bf16[1024,512]{1,0:T(8,128)(2,1)} %param.14) | copy-start | bytes 3145732
  576.3 5.2 copy-start.5
Sparse Core Ops, SparseCore 0:
  28.2 52.8 all-gather.2
  217.6 47.8 all-gather.4
  414.0 162.2 all-reduce.15
where the time goes:
time: 596 us; the launch traced here: 590 us
  waiting for transfers between devices  169 us (28%)
  blocking collectives  155 us (26%)
  local copies, waits for them, and re-layouts  143 us (24%)
  matrix products  64.2 us (11%)
  other arithmetic  23.4 us (4%)
  starting transfers between devices  20.7 us (3%)
  between operations  14.6 us (2%)
    all_gather x2, waiting for transfers between devices, collect(): lax.all_gather(values, 'wide', axis=0, tiled=True)  96.2 us
    all_to_all x1, blocking collectives, sum_at_owner(): pieces = lax.all_to_all(split_up(x, dim, length), axis, 0, 0, tiled=True)  78 us
    psum x1, blocking collectives, local(): lax.psum((conv_grad, down_grad, up_grad, class_grad), ('wide', 'samp'))  77 us
    psum x1, waiting for transfers between devices, local(): lax.psum((conv_grad, down_grad, up_grad, class_grad), ('wide', 'samp'))  69.6 us
    unnamed x88, local copies, waits for them, and re-layouts  43.5 us
    concatenate x6, local copies, waits for them, and re-layouts, taps_in(): jnp.concatenate([padded[p:p + height, q:q + across] for p in range(3) for...  24.7 us
    dot_general x2, matrix products, conv_padded(): jnp.dot(flattened, stacked, preferred_element_type=jnp.float32)  19.8 us
    dot_general x3, matrix products, conv_padded(): jnp.dot(window, weight.reshape(9 * inward, outward), preferred_element_ty...  18.2 us
  transfers between devices with their start and end apart: 8, of which 4 were waited for; matrix products, arithmetic and copies ran while one was open for 18% of the time, Pallas kernels for 0%

commit v1 on v0

--- a/solution.py
+++ b/solution.py
@@ -136,7 +136,12 @@
 
 
 def collect(values, transform):
-    return transform(lax.all_gather(values, "wide", axis=0, tiled=True), jnp.int32(0))
+    return transform(
+        jnp.concatenate(
+            lax.all_to_all(jnp.stack([values] * lax.axis_size("wide")), "wide", 0, 0), axis=0
+        ),
+        jnp.int32(0),
+    )
 
 
 def spread_sum(term_rows, row_total):

time: 596 us -> 690 us (1.16)
  blocking collectives: 155 us -> 237 us
  local copies, waits for them, and re-layouts: 143 us -> 181 us
  waiting for transfers between devices: 169 us -> 141 us
  starting transfers between devices: 20.7 us -> 31.2 us
    all_gather x2 -> x0, waiting for transfers between devices: 96.2 us -> none  [collect(): lax.all_gather(values, 'wide', axis=0, tiled=True)]
    all_to_all x0 -> x1, blocking collectives: none -> 82.1 us  [collect(): lax.all_to_all(jnp.stack([values] * lax.axis_size('wide')), 'wide', 0, 0)]
    all_to_all x0 -> x1, waiting for transfers between devices: none -> 68.3 us  [collect(): lax.all_to_all(jnp.stack([values] * lax.axis_size('wide')), 'wide', 0, 0)]
    reshape x0 -> x2, local copies, waits for them, and re-layouts: none -> 20.5 us  [collect(): jnp.concatenate(lax.all_to_all(jnp.stack([values] * lax.axis_size('wide')...]
    all_to_all x0 -> x3, local copies, waits for them, and re-layouts: none -> 17.2 us  [collect(): lax.all_to_all(jnp.stack([values] * lax.axis_size('wide')), 'wide', 0, 0)]
    all_gather x2 -> x0, local copies, waits for them, and re-layouts: 12.7 us -> none  [collect(): lax.all_gather(values, 'wide', axis=0, tiled=True)]
    another operation x0 -> x2, local copies, waits for them, and re-layouts: none -> 12.4 us  [collect(): jnp.stack([values] * lax.axis_size('wide'))]
  transfers between devices with their start and end apart: 8 -> 7, of which waited for: 4 -> 3; matrix products, arithmetic and copies ran while one was open for 18% -> 16% of each run, Pallas kernels for 0% -> 0%
where the time goes in v1:
time: 690 us; the launch traced here: 684 us
  blocking collectives  237 us (34%)
  local copies, waits for them, and re-layouts  181 us (26%)
  waiting for transfers between devices  141 us (20%)
  matrix products  60.3 us (9%)
  starting transfers between devices  31.2 us (5%)
  other arithmetic  18.3 us (3%)
  between operations  14.9 us (2%)
    all_to_all x1, blocking collectives, collect(): lax.all_to_all(jnp.stack([values] * lax.axis_size('wide')), 'wide', 0, 0)  82.1 us
    all_to_all x1, blocking collectives, sum_at_owner(): pieces = lax.all_to_all(split_up(x, dim, length), axis, 0, 0, tiled=True)  78.1 us
    psum x1, blocking collectives, local(): lax.psum((conv_grad, down_grad, up_grad, class_grad), ('wide', 'samp'))  77.2 us
    psum x1, waiting for transfers between devices, local(): lax.psum((conv_grad, down_grad, up_grad, class_grad), ('wide', 'samp'))  69.4 us
    all_to_all x1, waiting for transfers between devices, collect(): lax.all_to_all(jnp.stack([values] * lax.axis_size('wide')), 'wide', 0, 0)  68.3 us
    unnamed x88, local copies, waits for them, and re-layouts  44.1 us
    concatenate x6, local copies, waits for them, and re-layouts, taps_in(): jnp.concatenate([padded[p:p + height, q:q + across] for p in range(3) for...  24.8 us
    dot_general x2, matrix products, conv_padded(): jnp.dot(flattened, stacked, preferred_element_type=jnp.float32)  21 us
  transfers between devices with their start and end apart: 7, of which 3 were waited for; matrix products, arithmetic and copies ran while one was open for 16% of the time, Pallas kernels for 0%

profile of v1, /device:TPU:1, one launch (start us, length us, event | category | flops | bytes accessed | tf_op | source)
XLA Modules:
  0.0 684.2 jit_solution(15252693164859389674)
XLA Ops:
  8.0 4.5 collective-permute-start
  12.5 1.9 collective-permute-start.1
  14.5 3.2 collective-permute-done.1
  18.7 1.6 constant_dynamic-update-slice_fusion.16
  21.3 1.6 constant_dynamic-update-slice_fusion.10
  23.7 2.0 multiply_convert_fusion.3
  25.9 1.5 convolution_convert_fusion.4
  27.6 5.8 stack.4
  33.4 82.1 %all_to_all.30 = bf16[32,2,48,1024]{3,1,2,0:T(2,128)(2,1)S(1)} all-to-all(bf16[32,2,48,1024]{3,1,2,0:T(2,128)(2,1)S(1)} %stack.4), channel_id=1, replica_groups=mesh['wide'=32,'samp'=4] {'wide'}, dimensions={0} | all-to-all | bytes 12582912 | tf_op jit(solution)/shard_map/all_to_all | solution.py:141
  115.5 5.3 copy.60
  120.9 10.3 %reshape.147 = bf16[64,48,1024]{2,0,1:T(8,128)(2,1)} reshape(bf16[32,2,48,1024]{3,1,0,2:T(2,128)(2,1)} %copy.60) | data formatting | bytes 12582912 | tf_op jit(solution)/shard_map/reshape | solution.py:140
  131.1 10.3 %fusion.1 = f32[66,50,9,64]{0,3,2,1:T(8,128)S(1)} fusion(bf16[9,64,1024,1]{2,1,0,3:T(8,128)(2,1)S(1)} %bitcast.180, bf16[64,48,1024]{2,0,1:T(8,128)(2,1)} %reshape.147), kind=kOutput, calls=%fused_computation.3 | convolution fusion | flops 3892838400 | bytes 15074304 | tf_op jit(solution)/shard_map/dot_general | solution.py:79
  141.5 2.5 multiply_convert_fusion
  144.0 1.3 slice_dynamic-update-slice_fusion.15
  146.5 1.3 slice_dynamic-update-slice_fusion.13
  152.3 1.2 slice_dynamic-update-slice_fusion.9
  153.6 1.2 slice_dynamic-update-slice_fusion.8
  154.8 10.7 %copy.61 = bf16[64,48,576]{2,1,0:T(8,128)(2,1)} copy(bf16[64,48,576]{0,2,1:T(8,128)(2,1)} %slice_dynamic-update-slice_fusion.8) | data formatting | bytes 7077888 | tf_op jit(solution)/shard_map/concatenate | solution.py:54
  165.5 7.1 %convolution_convert_fusion.1 = bf16[64,48,1024]{2,1,0:T(8,128)(2,1)S(1)} fusion(bf16[64,48,576]{2,1,0:T(8,128)(2,1)} %copy.61, bf16[576,1024,1]{1,0,2:T(8,128)(2,1)} %bitcast.181), kind=kOutput, calls=%fused_computation.11 | convolution fusion | flops 3627024384 | bytes 11010048 | tf_op jit(solution)/shard_map/dot_general | solution.py:73
  172.6 78.1 %all_to_all.31 = bf16[32,2,48,1024]{3,2,1,0:T(8,128)(2,1)S(1)} all-to-all(bf16[32,2,48,1024]{3,2,1,0:T(8,128)(2,1)S(1)} %bitcast.170), channel_id=1, replica_groups=mesh['wide'=32,'samp'=4] {'wide'}, dimensions={0} | all-to-all | bytes 12582912 | tf_op jit(solution)/shard_map/all_to_all | solution.py:15
  250.8 1.5 convert_reduce_fusion.1
  255.1 6.6 stack.5
  261.7 4.9 all-to-all-start.2
  266.6 2.4 rev.7
  269.0 2.4 rev.6
  271.4 68.3 %all-to-all-done.2 = bf16[32,2,48,1024]{3,1,2,0:T(2,128)(2,1)} async-done(((bf16[32,2,48,1024]{3,1,2,0:T(2,128)(2,1)}), bf16[32,2,48,1024]{3,1,2,0:T(2,128)(2,1)}, u32[]{:S(2)}, u32[]{:S(2)}) %all-to-all-start.2) | async-done | bytes 6291488 | tf_op jit(solution)/shard_map/all_to_all | solution.py:141
  339.7 6.8 copy.65
  346.4 10.2 %reshape.155 = bf16[64,48,1024]{2,0,1:T(8,128)(2,1)} reshape(bf16[32,2,48,1024]{3,1,0,2:T(2,128)(2,1)} %copy.65) | data formatting | bytes 12582912 | tf_op jit(solution)/shard_map/reshape | solution.py:140
  356.7 10.7 %fusion.3 = f32[66,50,9,64]{0,3,1,2:T(8,128)S(1)} fusion(bf16[9,64,1024,1]{2,1,3,0:T(8,128)(2,1)} %bitcast.183, bf16[64,48,1024]{2,0,1:T(8,128)(2,1)} %reshape.155), kind=kOutput, calls=%fused_computation.5 | convolution fusion | flops 3892838400 | bytes 15074304 | tf_op jit(solution)/shard_map/dot_general | solution.py:79
  367.3 2.6 fusion.10
  370.0 1.3 slice_dynamic-update-slice_fusion.7
  371.2 1.3 slice_dynamic-update-slice_fusion.6
  377.0 1.2 slice_dynamic-update-slice_fusion.2
  379.4 1.3 slice_dynamic-update-slice_fusion
  380.7 10.7 %copy.75 = bf16[64,48,576]{2,1,0:T(8,128)(2,1)} copy(bf16[64,48,576]{0,2,1:T(8,128)(2,1)} %slice_dynamic-update-slice_fusion) | data formatting | bytes 7077888 | tf_op jit(solution)/shard_map/concatenate | solution.py:54
  391.4 9.0 %convolution_convert_fusion = bf16[64,48,1024]{2,1,0:T(8,128)(2,1)} fusion(bf16[64,48,576]{2,1,0:T(8,128)(2,1)} %copy.75, bf16[576,1024,1]{1,0,2:T(8,128)(2,1)S(1)} %bitcast.182), kind=kOutput, calls=%fused_computation.10 | convolution fusion | flops 3627024384 | bytes 11010048 | tf_op jit(solution)/shard_map/dot_general | solution.py:73
  400.5 10.3 %all-to-all-start.3 = ((bf16[32,2,48,1024]{3,2,1,0:T(8,128)(2,1)}), bf16[32,2,48,1024]{3,2,1,0:T(8,128)(2,1)}, u32[]{:S(2)}, u32[]{:S(2)}) async-start(bf16[32,2,48,1024]{3,2,1,0:T(8,128)(2,1)} %bitcast.168), calls=%async_computation.3 | async-start | bytes 12582912 | tf_op jit(solution)/shard_map/all_to_all | solution.py:15
  412.7 6.3 copy.97
  419.0 7.7 %pad.52.clone = bf16[66,50,1024]{2,1,0:T(8,128)(2,1)} pad(bf16[64,48,1024]{2,1,0:T(8,128)(2,1)S(1)} %copy.97, bf16[]{:T(256)} %constant.4.clone.1), padding=1_1x1_1x0_0 | pad | bytes 13049858 | tf_op jit(solution)/shard_map/jit(_pad)/pad | solution.py:38
  426.7 9.4 %reshape.188 = bf16[3300,1024,1,1]{1,0,2,3:T(8,128)(2,1)} reshape(bf16[66,50,1024]{2,1,0:T(8,128)(2,1)} %pad.52.clone) | data formatting | bytes 13516800 | tf_op jit(solution)/shard_map/reshape | solution.py:77
  436.1 6.3 copy.82
  442.4 1.8 fusion.50
  444.2 5.1 copy.83
  449.3 3.9 convolution_convert_fusion.2
  454.4 1.2 pad_dynamic-update-slice_fusion.7
  457.9 1.3 pad_dynamic-update-slice_fusion.4
  459.2 1.3 pad_dynamic-update-slice_fusion.8
  460.4 1.3 pad_dynamic-update-slice_fusion.3
  461.7 1.3 pad_dynamic-update-slice_fusion.2
  463.0 1.3 pad_dynamic-update-slice_fusion.1
  464.3 1.2 pad_dynamic-update-slice_fusion
  465.5 12.9 %copy.78 = bf16[66,50,576]{2,1,0:T(8,128)(2,1)} copy(bf16[66,50,576]{0,2,1:T(8,128)(2,1)} %pad_dynamic-update-slice_fusion) | data formatting | bytes 7603200 | tf_op jit(solution)/shard_map/concatenate | solution.py:60
  478.4 7.9 %reshape.164 = bf16[3300,576]{1,0:T(8,128)(2,1)} reshape(bf16[66,50,576]{2,1,0:T(8,128)(2,1)} %copy.78) | data formatting | bytes 7603200 | tf_op jit(solution)/shard_map/reshape | solution.py:102
  486.3 6.3 copy.79
  492.6 5.2 all-to-all-start.5
  498.0 4.3 convert_reduce_fusion
  505.4 2.7 fusion.49
  508.1 8.2 %fusion.12 = bf16[1024,3,3,64]{0,3,2,1:T(8,128)(2,1)S(1)} fusion(bf16[3,3,64,3300]{3,2,1,0:T(8,128)(2,1)} %bitcast.171, bf16[3300,1024,1,1]{1,0,2,3:T(8,128)(2,1)} %reshape.188), kind=kOutput, calls=%fused_computation.36 | convolution fusion | flops 3893428224 | bytes 11739648 | tf_op jit(solution)/shard_map/dot_general | solution.py:103
  517.5 4.2 all-to-all-start.4
  521.9 77.2 %psum.31 = f32[128,9]{0,1:T(8,128)} all-reduce(f32[128,9]{0,1:T(8,128)S(1)} %convolution_bitcast_fusion), channel_id=1, replica_groups=mesh['wide'=32,'samp'=4] {'wide','samp'}, use_global_device_ids=true, to_apply=%region_8.9 | all-reduce | flops 1152 | bytes 9216 | tf_op jit(solution)/shard_map/psum | solution.py:223
  601.1 69.4 %all-reduce.16.cloned.1.call-done = (f32[3,3,128,128]{3,2,1,0:T(8,128)}, f32[512,1024]{1,0:T(8,128)}, f32[1024,512]{1,0:T(8,128)}) async-done(((f32[3,3,128,128]{3,2,1,0:T(8,128)}, f32[512,1024]{1,0:T(8,128)}, f32[1024,512]{1,0:T(8,128)}), (f32[3,3,128,128]{3,2,1,0:T(8,128)}, f32[512,1024]{1,0:T(8,128)}, f32[1024,512]{1,0:T(8,128)})) %all-reduce.16.cloned.1.call-update) | async-done | bytes 4784144 | tf_op jit(solution)/shard_map/psum | solution.py:223
  670.5 2.1 copy.145
  672.6 3.2 copy.146
  675.7 1.3 copy.147
  (110 shorter events, 30.4 us)
Async XLA Ops:
  7.2 245.2 %copy-start = (bf16[1024,512]{1,0:T(8,128)(2,1)S(1)}, bf16[1024,512]{1,0:T(8,128)(2,1)}, u32[]{:S(2)}) copy-start(bf16[1024,512]{1,0:T(8,128)(2,1)} %param.14) | copy-start | bytes 3145732
  8.0 6.4 collective-permute-start
  12.5 5.1 collective-permute-start.1
  120.9 10.3 %copy-start.6 = (bf16[3,3,1024,64]{2,3,1,0:T(8,128)(2,1)S(1)}, bf16[3,3,1024,64]{2,3,1,0:T(8,128)(2,1)}, u32[]{:S(2)}) copy-start(bf16[3,3,1024,64]{2,3,1,0:T(8,128)(2,1)} %param.12) | copy-start | bytes 3538948
  250.8 2.2 copy-start.21
  250.8 2.8 copy-start.22
  253.0 0.6 copy-start.19
  253.8 0.6 copy-start.10
  253.9 7.8 %copy-start.8 = (bf16[2,2,48,2,128]{4,3,1,2,0:T(2,128)(2,1)}, bf16[2,2,48,2,128]{4,3,1,2,0:T(2,128)(2,1)S(1)}, u32[]{:S(2)}) copy-start(bf16[2,2,48,2,128]{4,3,1,2,0:T(2,128)(2,1)S(1)} %copy.100) | copy-start | bytes 294916
  261.7 77.9 %all-to-all-start.2 = ((bf16[32,2,48,1024]{3,1,2,0:T(2,128)(2,1)}), bf16[32,2,48,1024]{3,1,2,0:T(2,128)(2,1)}, u32[]{:S(2)}, u32[]{:S(2)}) async-start(bf16[32,2,48,1024]{3,1,2,0:T(2,128)(2,1)} %stack.5), calls=%async_computation.2 | async-start | bytes 12582912 | tf_op jit(solution)/shard_map/all_to_all | solution.py:141
  379.4 11.9 %copy-start.7 = (bf16[3,3,1024,64]{2,3,1,0:T(8,128)(2,1)S(1)}, bf16[3,3,1024,64]{2,3,1,0:T(8,128)(2,1)}, u32[]{:S(2)}) copy-start(bf16[3,3,1024,64]{2,3,1,0:T(8,128)(2,1)} %rev.7) | copy-start | bytes 3538948
  400.4 11.0 %copy-start.16 = (bf16[4,96,128]{2,1,0:T(8,128)(2,1)S(1)}, bf16[4,96,128]{2,1,0:T(8,128)(2,1)}, u32[]{:S(2)}) copy-start(bf16[4,96,128]{2,1,0:T(8,128)(2,1)} %get-tuple-element.20) | copy-start | bytes 294916
  400.4 11.1 %copy-start.18 = (bf16[4,96,128]{2,1,0:T(8,128)(2,1)S(1)}, bf16[4,96,128]{2,1,0:T(8,128)(2,1)}, u32[]{:S(2)}) copy-start(bf16[4,96,128]{2,1,0:T(8,128)(2,1)} %get-tuple-element.14) | copy-start | bytes 294916
  400.4 11.1 %copy-start.15 = (bf16[4,96,128]{2,1,0:T(8,128)(2,1)S(1)}, bf16[4,96,128]{2,1,0:T(8,128)(2,1)}, u32[]{:S(2)}) copy-start(bf16[4,96,128]{2,1,0:T(8,128)(2,1)} %get-tuple-element.19) | copy-start | bytes 294916
  400.4 11.1 %copy-start.14 = (bf16[4,96,128]{2,1,0:T(8,128)(2,1)S(1)}, bf16[4,96,128]{2,1,0:T(8,128)(2,1)}, u32[]{:S(2)}) copy-start(bf16[4,96,128]{2,1,0:T(8,128)(2,1)} %get-tuple-element.18) | copy-start | bytes 294916
  400.4 11.2 %copy-start.4 = (bf16[1,4,96,128]{3,2,1,0:T(8,128)(2,1)S(1)}, bf16[1,4,96,128]{3,2,1,0:T(8,128)(2,1)}, u32[]{:S(2)}) copy-start(bf16[1,4,96,128]{3,2,1,0:T(8,128)(2,1)} %param.8) | copy-start | bytes 294916
  400.5 11.2 %copy-start.13 = (bf16[4,96,128]{2,1,0:T(8,128)(2,1)S(1)}, bf16[4,96,128]{2,1,0:T(8,128)(2,1)}, u32[]{:S(2)}) copy-start(bf16[4,96,128]{2,1,0:T(8,128)(2,1)} %get-tuple-element.17) | copy-start | bytes 294916
  400.5 11.2 %copy-start.12 = (bf16[4,96,128]{2,1,0:T(8,128)(2,1)S(1)}, bf16[4,96,128]{2,1,0:T(8,128)(2,1)}, u32[]{:S(2)}) copy-start(bf16[4,96,128]{2,1,0:T(8,128)(2,1)} %get-tuple-element.16) | copy-start | bytes 294916
  400.5 11.3 %copy-start.17 = (bf16[4,96,128]{2,1,0:T(8,128)(2,1)S(1)}, bf16[4,96,128]{2,1,0:T(8,128)(2,1)}, u32[]{:S(2)}) copy-start(bf16[4,96,128]{2,1,0:T(8,128)(2,1)} %get-tuple-element.12) | copy-start | bytes 294916
  400.5 11.3 %copy-start.11 = (bf16[4,96,128]{2,1,0:T(8,128)(2,1)S(1)}, bf16[4,96,128]{2,1,0:T(8,128)(2,1)}, u32[]{:S(2)}) copy-start(bf16[4,96,128]{2,1,0:T(8,128)(2,1)} %get-tuple-element.21) | copy-start | bytes 294916
  400.5 92.1 %all-to-all-start.3 = ((bf16[32,2,48,1024]{3,2,1,0:T(8,128)(2,1)}), bf16[32,2,48,1024]{3,2,1,0:T(8,128)(2,1)}, u32[]{:S(2)}, u32[]{:S(2)}) async-start(bf16[32,2,48,1024]{3,2,1,0:T(8,128)(2,1)} %bitcast.168), calls=%async_computation.3 | async-start | bytes 12582912 | tf_op jit(solution)/shard_map/all_to_all | solution.py:15
  436.1 6.3 copy-start.9
  444.2 5.1 copy-start.3
  492.6 9.8 %copy-start.2 = (bf16[512,1024]{1,0:T(8,128)(2,1)S(1)}, bf16[512,1024]{1,0:T(8,128)(2,1)}, u32[]{:S(2)}) copy-start(bf16[512,1024]{1,0:T(8,128)(2,1)} %param.11) | copy-start | bytes 3145732
  492.6 24.9 %all-to-all-start.5 = ((bf16[4,3,3,64,256]{4,3,2,1,0:T(8,128)(2,1)}), bf16[4,3,3,64,256]{4,3,2,1,0:T(8,128)(2,1)S(1)}, u32[]{:S(2)}, u32[]{:S(2)}) async-start(bf16[4,3,3,64,256]{4,3,2,1,0:T(8,128)(2,1)} %bitcast.161), calls=%async_computation.5 | async-start | bytes 2359296 | tf_op jit(solution)/shard_map/all_to_all | solution.py:15
  497.7 172.8 %all-reduce.16.cloned.1.call-start = ((), (), s32[]{:S(2)}) async-start(), calls=%async_computation.6 | async-start | bytes 9568256 | tf_op jit(solution)/shard_map/psum | solution.py:223
  508.1 13.6 %copy-start.20 = (bf16[4,96,128]{2,1,0:T(8,128)(2,1)S(1)}, bf16[4,96,128]{2,1,0:T(8,128)(2,1)}, u32[]{:S(2)}) copy-start(bf16[4,96,128]{2,1,0:T(8,128)(2,1)} %copy-done.19) | copy-start | bytes 294916
  517.5 82.6 %all-to-all-start.4 = ((bf16[4,3,3,256,64]{3,4,2,1,0:T(8,128)(2,1)}), bf16[4,3,3,256,64]{3,4,2,1,0:T(8,128)(2,1)S(1)}, u32[]{:S(2)}, u32[]{:S(2)}) async-start(bf16[4,3,3,256,64]{3,4,2,1,0:T(8,128)(2,1)} %bitcast.163), calls=%async_computation.4 | async-start | bytes 2359296 | tf_op jit(solution)/shard_map/all_to_all | solution.py:15
  521.9 155.1 %copy-start.1 = (bf16[1024,512]{1,0:T(8,128)(2,1)S(1)}, bf16[1024,512]{1,0:T(8,128)(2,1)}, u32[]{:S(2)}) copy-start(bf16[1024,512]{1,0:T(8,128)(2,1)} %param.14) | copy-start | bytes 3145732
  670.5 5.2 copy-start.5
Sparse Core Ops, SparseCore 0:
  508.2 162.2 all-reduce.15
